TPU v7x, 32 devices: a whole 2x2x4 slice. The times are simulated.
32 devices in a mesh: tm: 8 (over z, core), cell: 4 (over y, x).
Axes of the slice: x: 2, y: 2, z: 4, core: 2. Of those that a mesh axis runs over, the one named last changes fastest.
Arguments:
- points: float32 [8, 30, 2048], P('tm', None, 'cell')
- last_points: float32 [30, 2048], P(None, 'cell'), may hold values from -5 to 5
- counts: int32 [9], replicated, may hold values from 512 to 2048
- bins: int32 [8, 2048], P('tm', 'cell'), may hold values from 0 to 15
- rates: float32 [8, 16], P('tm'), may hold values from 0.25 to 4
Outputs:
- source_potential: float32 [8, 2048], P('tm', 'cell')
- target_potential: float32 [8, 2048], P('tm', 'cell')
- ancestor_mass: float32 [8, 2048], P('tm', 'cell')
All inputs are finite; a program needn't handle non-finite values.
Results may differ from a plain program's by a relative error of at most 0.0003.
Values sent between devices are 32-bit elements; how exact they have to be, the bound alone decides.
A program may use at most 64 MiB of HBM per device.

v0:
```python
import jax
import jax.numpy as jnp
from jax import lax
from jax.sharding import PartitionSpec as P

ITERS = 4


EPS = 0.05
FI = 1.0 / 1.05
FJ = 50.0 / 50.05
NEG = -1e30


def from_behind(shard, axis, by):
    length = lax.axis_size(axis)
    pairs = [(i, i + by) for i in range(length) if 0 <= i + by < length]
    return lax.ppermute(shard, axis, pairs)


def joined(value, axis, join):
    pieces = jax.tree.map(lambda part: lax.all_gather(part, axis), value)
    head = jax.tree.map(lambda part: part[0], pieces)
    tail = jax.tree.map(lambda part: part[1:], pieces)
    total, _ = lax.scan(lambda total, share: (join(total, share), None), head, tail)
    return total


def combine(first, second):
    top = jnp.maximum(first[0], second[0])
    return (top, first[1] * jnp.exp(first[0] - top) + second[1] * jnp.exp(second[0] - top))


def local(points, last_points, counts, bins, rates):
    cell_dev = points.shape[2]
    cells = cell_dev * lax.axis_size("cell")
    tm_pos = lax.axis_index("tm")
    cell_pos = lax.axis_index("cell")
    source = points[0]
    shifted = from_behind(source, "tm", -1)
    target = jnp.where(tm_pos == lax.axis_size("tm") - 1, last_points, shifted)
    targets = lax.all_gather(target, "cell", axis=1, tiled=True)
    nsrc = counts[tm_pos]
    ntgt = counts[tm_pos + 1]
    own_index = cell_pos * cell_dev + jnp.arange(cell_dev, dtype=jnp.int32)
    live_rows = own_index < nsrc
    live_cols = jnp.arange(cells, dtype=jnp.int32) < ntgt
    table = bins[0][None, :] == jnp.arange(rates.shape[1], dtype=jnp.int32)[:, None]
    growth = jnp.sum(jnp.where(table, rates[0][:, None], 0.0), axis=0)
    blk = min(128, cell_dev)
    nblocks = cell_dev // blk
    sqx = jnp.sum(source * source, axis=0)
    sqy = jnp.sum(targets * targets, axis=0)
    blocks_x = source.reshape(source.shape[0], nblocks, blk).transpose(1, 0, 2)
    blocks_sq = sqx.reshape(nblocks, blk)
    blocks_live = live_rows.reshape(nblocks, blk)

    def raw_cost(xblock, sqblock):
        cross = jnp.dot(xblock.T, targets, precision=lax.Precision.HIGHEST)
        return sqblock[:, None] + sqy[None, :] - 2.0 * cross

    def block_total(item):
        xblock, sqblock, liveblock = item
        both = liveblock[:, None] & live_cols[None, :]
        return jnp.sum(jnp.where(both, raw_cost(xblock, sqblock), 0.0))

    cost_part = jnp.sum(lax.map(block_total, (blocks_x, blocks_sq, blocks_live)))
    growth_part = jnp.sum(jnp.where(live_rows, growth, 0.0))
    growth_sum = lax.psum(growth_part, "cell")
    cost_sum = lax.psum(cost_part, "cell")
    cbar = cost_sum / (nsrc.astype(jnp.float32) * ntgt.astype(jnp.float32))
    gbar = growth_sum / nsrc.astype(jnp.float32)
    loga = jnp.log(growth) - jnp.log(gbar)

    def row_lse(row_terms, hfull):

        def row_one_block(item):
            xblock, sqblock, termblock = item
            scaled = raw_cost(xblock, sqblock) / cbar
            score = jnp.where(
                live_cols[None, :], (termblock[:, None] + hfull[None, :] - scaled) / EPS, NEG
            )
            top = jnp.max(score, axis=1)
            return top + jnp.log(jnp.sum(jnp.exp(score - top[:, None]), axis=1))

        return lax.map(
            row_one_block, (blocks_x, blocks_sq, row_terms.reshape(nblocks, blk))
        ).reshape(cell_dev)

    zero_rows = jnp.zeros((cell_dev,), jnp.float32)
    hfull = jnp.zeros((cells,), jnp.float32)
    fpot = zero_rows
    for step in range(ITERS):
        fpot = jnp.where(live_rows, FI * (EPS * loga - EPS * row_lse(zero_rows, hfull)), 0.0)

        def column_one_block(carry, item):
            xblock, sqblock, fblock, liveblock = item
            scaled = raw_cost(xblock, sqblock) / cbar
            score = jnp.where(liveblock[:, None], (fblock[:, None] - scaled) / EPS, NEG)
            top = jnp.maximum(carry[0], jnp.max(score, axis=0))
            total = carry[1] * jnp.exp(carry[0] - top) + jnp.sum(
                jnp.exp(score - top[None, :]), axis=0
            )
            return ((top, total), None)

        start = (jnp.full((cells,), NEG, jnp.float32), jnp.zeros((cells,), jnp.float32))
        carry, unused = lax.scan(
            column_one_block, start, (blocks_x, blocks_sq, fpot.reshape(nblocks, blk), blocks_live)
        )
        partial_top, partial_total = carry
        top, total = joined((partial_top, partial_total), "cell", combine)
        hfull = jnp.where(live_cols, FJ * (-EPS * (top + jnp.log(total))), 0.0)
    hown = lax.dynamic_slice_in_dim(hfull, cell_pos * cell_dev, cell_dev, 0)
    mass = jnp.where(live_rows, jnp.exp(row_lse(fpot, hfull)), 0.0)
    return (fpot[None], hown[None], mass[None])


def solution(mesh):
    return jax.shard_map(
        local,
        mesh=mesh,
        in_specs=(P("tm", None, "cell"), P(None, "cell"), P(), P("tm", "cell"), P("tm", None)),
        out_specs=(P("tm", "cell"), P("tm", "cell"), P("tm", "cell")),
        check_vma=False,
    )
```

profile of v0, /device:TPU:0, one launch (start us, length us, event | category | flops | bytes accessed | tf_op | source)
XLA Modules:
  0.0 193.5 jit_solution(5489789511784782073)
XLA Ops:
  8.2 10.8 %all_gather.51 = f32[30,2048]{1,0:T(8,128)S(1)} all-gather(f32[30,512]{1,0:T(8,128)S(1)} %broadcast_select_fusion), channel_id=1, replica_groups=mesh['tm'=8,'cell'=4] {'cell'}, dimensions={1}, use_global_device_ids=true | all-gather | bytes 307200 | tf_op jit(solution)/shard_map/all_gather | solution.py:42
  19.0 13.0 %while.170 = (s32[]{:T(128)}, f32[4]{0:T(128)S(1)}, pred[4,128]{1,0:T(4,128)(4,1)S(1)}, f32[4,128]{1,0:T(4,128)S(1)}, f32[2048]{0:T(1024)S(1)}, /*index=5*/f32[4...) while((s32[]{:T(128)}, f32[4]{0:T(128)S(1)}, pred[4,128]{1,0:T(4,128)(4,1)S(1)}, ...), condition=%wide.region_7.8_spmd.clone, body=%wide.region_5.7_spmd.clone.sunk | while | flops 95946752 | bytes 293245 | solution.py:67
  19.7 1.9 fusion.167
  22.9 1.9 fusion.167
  26.2 1.9 fusion.167
  29.4 1.9 fusion.167
  32.8 9.6 %all-reduce = (f32[]{:T(128)}, f32[]{:T(128)}) all-reduce(f32[]{:T(128)} %select_reduce_fusion.1, f32[]{:T(128)} %reduce_sum.139), channel_id=1, replica_groups=mesh['tm'=8,'cell'=4] {'cell'}, use_global_device_ids=true, to_apply=%region_2.3 | all-reduce | flops 2 | bytes 16 | tf_op jit(solution)/shard_map/psum | solution.py:69
  43.7 9.2 %while.171 = (s32[]{:T(128)}, f32[4,128]{1,0:T(4,128)S(1)}, f32[4,128]{1,0:T(4,128)S(1)}, f32[2048]{0:T(1024)S(1)}, f32[4,30,128]{2,1,0:T(8,128)S(1)}, /*index=5...) while((s32[]{:T(128)}, f32[4,128]{1,0:T(4,128)S(1)}, ...), condition=%wide.region_13.14_spmd.clone, body=%wide.region_10.13_spmd.clone.sunk | while | flops 96995200 | bytes 2393721 | solution.py:86
  53.5 6.2 %while.176 = (s32[]{:T(128)}, f32[2048]{0:T(1024)S(1)}, f32[2048]{0:T(1024)S(1)}, pred[4,128]{1,0:T(4,128)(4,1)S(1)}, f32[4,128]{1,0:T(4,128)S(1)}, /*index=5*/f...) while((s32[]{:T(128)}, f32[2048]{0:T(1024)S(1)}, ...), condition=%wide.region_17.18_spmd.clone, body=%wide.region_14.17_spmd.clone.sunk | while | flops 97003520 | bytes 2494352 | solution.py:107
  59.7 8.1 %all-gather = f32[8192]{0:T(1024)S(1)} all-gather(f32[2048]{0:T(1024)S(1)} %get-tuple-element.606), channel_id=2, replica_groups=mesh['tm'=8,'cell'=4] {'cell'}, dimensions={0}, use_global_device_ids=true | all-gather | bytes 40960 | tf_op jit(solution)/shard_map/all_gather | solution.py:22
  68.5 7.2 %all-gather.1 = f32[8192]{0:T(1024)S(1)} all-gather(f32[2048]{0:T(1024)S(1)} %get-tuple-element.607), channel_id=3, replica_groups=mesh['tm'=8,'cell'=4] {'cell'}, dimensions={0}, use_global_device_ids=true | all-gather | bytes 40960 | tf_op jit(solution)/shard_map/all_gather | solution.py:22
  78.6 9.2 %while.172 = (s32[]{:T(128)}, f32[4,128]{1,0:T(4,128)S(1)}, f32[2048]{0:T(1024)S(1)}, f32[4,128]{1,0:T(4,128)S(1)}, f32[2048]{0:T(1024)S(1)}, /*index=5*/f32[4,3...) while((s32[]{:T(128)}, f32[4,128]{1,0:T(4,128)S(1)}, ...), condition=%wide.region_23.24_spmd.clone, body=%wide.region_20.23_spmd.clone.sunk | while | flops 96995200 | bytes 2401921 | solution.py:86
  88.5 6.2 %while.177 = (s32[]{:T(128)}, f32[2048]{0:T(1024)S(1)}, f32[2048]{0:T(1024)S(1)}, pred[4,128]{1,0:T(4,128)(4,1)S(1)}, f32[4,128]{1,0:T(4,128)S(1)}, /*index=5*/f...) while((s32[]{:T(128)}, f32[2048]{0:T(1024)S(1)}, ...), condition=%wide.region_27.28_spmd.clone, body=%wide.region_24.27_spmd.clone.sunk | while | flops 97003520 | bytes 2494352 | solution.py:107
  94.7 8.1 %all-gather.2 = f32[8192]{0:T(1024)S(1)} all-gather(f32[2048]{0:T(1024)S(1)} %get-tuple-element.611), channel_id=4, replica_groups=mesh['tm'=8,'cell'=4] {'cell'}, dimensions={0}, use_global_device_ids=true | all-gather | bytes 40960 | tf_op jit(solution)/shard_map/all_gather | solution.py:22
  103.4 7.2 %all-gather.3 = f32[8192]{0:T(1024)S(1)} all-gather(f32[2048]{0:T(1024)S(1)} %get-tuple-element.612), channel_id=5, replica_groups=mesh['tm'=8,'cell'=4] {'cell'}, dimensions={0}, use_global_device_ids=true | all-gather | bytes 40960 | tf_op jit(solution)/shard_map/all_gather | solution.py:22
  112.9 9.2 %while.173 = (s32[]{:T(128)}, f32[4,128]{1,0:T(4,128)S(1)}, f32[2048]{0:T(1024)S(1)}, f32[4,128]{1,0:T(4,128)S(1)}, f32[2048]{0:T(1024)S(1)}, /*index=5*/f32[4,3...) while((s32[]{:T(128)}, f32[4,128]{1,0:T(4,128)S(1)}, ...), condition=%wide.region_33.34_spmd.clone, body=%wide.region_30.33_spmd.clone.sunk | while | flops 96995200 | bytes 2401921 | solution.py:86
  122.7 6.2 %while.178 = (s32[]{:T(128)}, f32[2048]{0:T(1024)S(1)}, f32[2048]{0:T(1024)S(1)}, pred[4,128]{1,0:T(4,128)(4,1)S(1)}, f32[4,128]{1,0:T(4,128)S(1)}, /*index=5*/f...) while((s32[]{:T(128)}, f32[2048]{0:T(1024)S(1)}, ...), condition=%wide.region_37.38_spmd.clone, body=%wide.region_34.37_spmd.clone.sunk | while | flops 97003520 | bytes 2494352 | solution.py:107
  128.9 8.1 %all-gather.4 = f32[8192]{0:T(1024)S(1)} all-gather(f32[2048]{0:T(1024)S(1)} %get-tuple-element.616), channel_id=6, replica_groups=mesh['tm'=8,'cell'=4] {'cell'}, dimensions={0}, use_global_device_ids=true | all-gather | bytes 40960 | tf_op jit(solution)/shard_map/all_gather | solution.py:22
  137.6 7.4 %all-gather.5 = f32[8192]{0:T(1024)S(1)} all-gather(f32[2048]{0:T(1024)S(1)} %get-tuple-element.617), channel_id=7, replica_groups=mesh['tm'=8,'cell'=4] {'cell'}, dimensions={0}, use_global_device_ids=true | all-gather | bytes 40960 | tf_op jit(solution)/shard_map/all_gather | solution.py:22
  147.3 9.2 %while.174 = (s32[]{:T(128)}, f32[4,128]{1,0:T(4,128)S(1)}, f32[2048]{0:T(1024)S(1)}, f32[4,128]{1,0:T(4,128)S(1)}, f32[2048]{0:T(1024)S(1)}, /*index=5*/f32[4,3...) while((s32[]{:T(128)}, f32[4,128]{1,0:T(4,128)S(1)}, ...), condition=%wide.region_43.44_spmd.clone, body=%wide.region_40.43_spmd.clone.sunk | while | flops 96995200 | bytes 2401921 | solution.py:86
  157.1 6.2 %while.179 = (s32[]{:T(128)}, f32[2048]{0:T(1024)S(1)}, f32[2048]{0:T(1024)S(1)}, pred[4,128]{1,0:T(4,128)(4,1)S(1)}, f32[4,128]{1,0:T(4,128)S(1)}, /*index=5*/f...) while((s32[]{:T(128)}, f32[2048]{0:T(1024)S(1)}, ...), condition=%wide.region_47.48_spmd.clone, body=%wide.region_44.47_spmd.clone.sunk | while | flops 97003520 | bytes 2494352 | solution.py:107
  163.3 8.1 %all-gather.6 = f32[8192]{0:T(1024)S(1)} all-gather(f32[2048]{0:T(1024)S(1)} %get-tuple-element.621), channel_id=8, replica_groups=mesh['tm'=8,'cell'=4] {'cell'}, dimensions={0}, use_global_device_ids=true | all-gather | bytes 40960 | tf_op jit(solution)/shard_map/all_gather | solution.py:22
  172.0 7.2 %all-gather.7 = f32[8192]{0:T(1024)S(1)} all-gather(f32[2048]{0:T(1024)S(1)} %get-tuple-element.622), channel_id=9, replica_groups=mesh['tm'=8,'cell'=4] {'cell'}, dimensions={0}, use_global_device_ids=true | all-gather | bytes 40960 | tf_op jit(solution)/shard_map/all_gather | solution.py:22
  182.9 9.4 %while.175 = (s32[]{:T(128)}, f32[4,128]{1,0:T(4,128)S(1)}, f32[4,128]{1,0:T(4,128)S(1)}, f32[2048]{0:T(1024)S(1)}, f32[4,128]{1,0:T(4,128)S(1)}, /*index=5*/f32...) while((s32[]{:T(128)}, f32[4,128]{1,0:T(4,128)S(1)}, ...), condition=%wide.region_53.54_spmd.clone, body=%wide.region_50.53_spmd.clone.sunk | while | flops 97257344 | bytes 2403465 | solution.py:86
  (377 shorter events, 99.1 us)
Async XLA Ops:
  0.6 2.2 %copy-start = (f32[1,30,512]{2,0,1:T(1,128)S(1)}, f32[1,30,512]{2,0,1:T(1,128)}, u32[]{:S(2)}) copy-start(f32[1,30,512]{2,0,1:T(1,128)} %param.33) | copy-start | bytes 184324
  1.5 6.6 %collective-permute-start = (f32[30,512]{1,0:T(8,128)S(1)}, f32[30,512]{1,0:T(8,128)S(1)}, u32[]{:S(2)}, u32[]{:S(2)}) collective-permute-start(f32[30,512]{1,0:T(8,128)S(1)} %bitcast.263), channel_id=1, source_target_pairs={{4,0},{8,4},{12,8},{16,12},{20,16},{24,20},{28,24},{5,1},{9,5},{13... | collective-permute-start | bytes 184328 | tf_op jit(solution)/shard_map/ppermute | solution.py:18
  3.0 5.2 %copy-start.9 = (f32[30,512]{1,0:T(8,128)S(1)}, f32[30,512]{1,0:T(8,128)}, u32[]{:S(2)}) copy-start(f32[30,512]{1,0:T(8,128)} %param.34) | copy-start | bytes 184324
  3.0 0.7 copy-start.10
  4.9 0.7 copy-start.11
  4.9 0.7 copy-start.12
  75.7 0.6 copy-start.5
  75.7 0.8 slice-start
  76.4 0.7 slice-start.8
  77.2 0.7 slice-start.1
  77.2 0.7 slice-start.9
  110.6 0.6 copy-start.6
  110.6 0.8 slice-start.2
  111.4 0.7 slice-start.3
  111.4 0.7 slice-start.10
  145.0 0.6 copy-start.7
  145.0 0.8 slice-start.4
  145.8 0.7 slice-start.5
  145.8 0.7 slice-start.11
  179.2 0.6 copy-start.8
  179.2 0.8 slice-start.6
  180.0 0.7 slice-start.12
  180.7 0.7 slice-start.7
  180.7 0.7 slice-start.13
  (4 other events, 2.4 us)
where the time goes:
time: 195 us; the launch traced here: 193 us
  blocking collectives  81.8 us (42%)
  matrix products  55.3 us (28%)
  other arithmetic  31.8 us (16%)
  local copies, waits for them, and re-layouts  17.8 us (9%)
  between operations  3.61 us (2%)
    all_gather x8, blocking collectives, joined(): pieces = jax.tree.map(lambda part: lax.all_gather(part, axis), value)  61.4 us
    dot_general x40, matrix products, raw_cost(): cross = jnp.dot(xblock.T, targets, precision=lax.Precision.HIGHEST)  55.3 us
    lt x24, other arithmetic, local(): live_cols = jnp.arange(cells, dtype=jnp.int32) < ntgt  13.6 us
    all_gather x1, blocking collectives, local(): targets = lax.all_gather(target, 'cell', axis=1, tiled=True)  10.8 us
    psum x1, blocking collectives, local(): growth_sum = lax.psum(growth_part, 'cell')  9.61 us
    unnamed x28, local copies, waits for them, and re-layouts  7.11 us
    reduce_sum x20, other arithmetic, row_one_block(): return top + jnp.log(jnp.sum(jnp.exp(score - top[:, None]), axis=1))  6.13 us
  transfers between devices with their start and end apart: 1, of which 0 were waited for; matrix products, arithmetic and copies ran while one was open for 1% of the time, Pallas kernels for 0%

commit v1 on v0

v1 whole, which is shorter than its diff:
```python
import functools
import math

import jax
import jax.numpy as jnp
from jax import lax
from jax.experimental import pallas as pl
from jax.experimental.pallas import tpu as pltpu
from jax.sharding import PartitionSpec as P

ITERS = 4

EPS = 0.05
FI = 1.0 / 1.05
FJ = 50.0 / 50.05
NEG = -1e30
LOG2E = math.log2(math.e)
UNIT = LOG2E / EPS

LANE = 128
SUB = 8
MESH = pl.DeviceIdType.MESH


def each(count, body):
    if count <= 4:
        for item in range(count):
            body(item)
    else:
        pl.loop(0, count)(body)


def tree(join, parts):
    while len(parts) > 1:
        parts = [join(*parts[i : i + 2]) if i + 1 < len(parts) else parts[i] for i in range(0, len(parts), 2)]
    return parts[0]


def splits(value):
    first = value.astype(jnp.bfloat16)
    rest = value - first.astype(jnp.float32)
    second = rest.astype(jnp.bfloat16)
    third = (rest - second.astype(jnp.float32)).astype(jnp.bfloat16)
    return first, second, third


def lane_totals(rows):
    part = tree(jnp.add, [rows[:, i : i + LANE] for i in range(0, rows.shape[1], LANE)])
    whole = jnp.concatenate([part, jnp.zeros((LANE - part.shape[0], LANE), jnp.float32)], axis=0)
    return jnp.sum(whole.T, axis=0, keepdims=True)


def kernel(nt, nc, points, last, counts, bins, rates, fout, hout, mout,
           cost, tgt, stats, parts, lhs, pot, row_max, row_sum, level, colpot,
           tgt_send, last_send, tgt_recv, st_send, st_recv, p_send, p_recv):
    t = lax.axis_index("tm")
    c = lax.axis_index("cell")
    pc, n = tgt.shape[1:]
    cells = nc * n
    tiles = n // SUB
    blocks = cells // LANE
    f32 = jnp.float32

    barrier = pltpu.get_barrier_semaphore()

    def peer(step):
        return lax.rem(c + step, nc)

    @pl.when(t < nt - 1)
    def _():
        for k in range(nc):
            pl.semaphore_signal(barrier, inc=1, device_id={"tm": t + 1, "cell": k}, device_id_type=MESH)

    for step in range(1, nc):
        pl.semaphore_signal(barrier, inc=1, device_id={"tm": t, "cell": peer(step)}, device_id_type=MESH)

    nsrc = counts[t]
    ntgt = counts[t + 1]
    mine = nsrc - c * n
    live = lax.broadcasted_iota(jnp.int32, (1, n), 1) < mine
    x = jnp.where(live, points[0], 0.0)
    sqx = jnp.sum(x * x, axis=0, keepdims=True)
    growth = jnp.zeros((1, n), f32)
    for k in range(rates.shape[1]):
        growth = jnp.where(bins[...] == k, rates[0, k], growth)
    stats[c] = lane_totals(jnp.concatenate([x, sqx, jnp.where(live, growth, 0.0)], axis=0))
    x1, x2, x3 = splits(jnp.concatenate([-2.0 * x, sqx, jnp.ones((1, n), f32)], axis=0))
    stacked = jnp.concatenate([x1, x1, x2, x2, x1, x3], axis=0)
    lhs[...] = stacked.T

    @pl.when(t == 0)
    def _():
        pl.semaphore_wait(barrier, nc - 1)

    @pl.when(t > 0)
    def _():
        pl.semaphore_wait(barrier, 2 * nc - 1)

    def stat_copy(step, slot):
        return pltpu.make_async_remote_copy(
            stats.at[slot], stats.at[slot], st_send.at[step], st_recv.at[slot],
            device_id={"tm": t, "cell": peer(step)}, device_id_type=MESH)

    def tgt_copy(step):
        return pltpu.make_async_remote_copy(
            points.at[0], tgt.at[c], tgt_send.at[step], tgt_recv.at[c],
            device_id={"tm": t - 1, "cell": peer(step)}, device_id_type=MESH)

    def last_copy(step):
        return pltpu.make_async_remote_copy(
            last, tgt.at[c], last_send.at[step], tgt_recv.at[c],
            device_id={"tm": t, "cell": peer(step)}, device_id_type=MESH)

    for step in range(1, nc):
        stat_copy(step, c).start()

    @pl.when(t > 0)
    def _():
        for step in range(nc):
            tgt_copy(step).start()

    @pl.when(t == nt - 1)
    def _():
        for step in range(1, nc):
            last_copy(step).start()
        pltpu.make_async_copy(last, tgt.at[c], tgt_recv.at[c]).start()

    for step in range(1, nc):
        stat_copy(step, peer(step)).wait_recv()
    source = tree(jnp.add, [stats[k] for k in range(nc)])
    lane = lax.broadcasted_iota(jnp.int32, (1, LANE), 1)

    def pick(row, index):
        return jnp.sum(jnp.where(lane == index, row, 0.0), axis=1, keepdims=True)

    nsrc_f = nsrc.astype(f32)
    ntgt_f = ntgt.astype(f32)
    gbar = pick(source, pc + 1) / nsrc_f
    loga = (jnp.log(growth) - jnp.log(gbar)) * LOG2E
    for k in range(n // LANE):
        wide = jnp.broadcast_to(loga[:, k * LANE : (k + 1) * LANE], (LANE, LANE))
        level[k * (LANE // SUB) : (k + 1) * (LANE // SUB)] = wide.T.reshape(LANE // SUB, SUB, LANE)

    colpot[...] = jnp.zeros_like(colpot)
    stats[nc] = jnp.zeros((1, LANE), f32)

    def take(step):
        k = peer(step)
        pltpu.make_async_copy(tgt.at[k], tgt.at[k], tgt_recv.at[k]).wait()
        ok = lax.broadcasted_iota(jnp.int32, (1, n), 1) < ntgt - k * n
        y = jnp.where(ok, tgt[k], 0.0)
        sqy = jnp.sum(y * y, axis=0, keepdims=True)
        one = jnp.ones((1, n), f32)
        stats[nc] += lane_totals(jnp.concatenate([y, sqy, jnp.zeros((1, n), f32)], axis=0))
        y1, y2, y3 = splits(jnp.concatenate([y, one, sqy], axis=0))
        rhs = jnp.concatenate([y1, y2, y1, y2, y3, y1], axis=0)
        cols = pl.ds(pl.multiple_of(k * n, LANE), n)
        for rb in range(n // LANE):
            got = jnp.dot(lhs[rb * LANE : (rb + 1) * LANE], rhs, preferred_element_type=f32)
            cost[rb * (LANE // SUB) : (rb + 1) * (LANE // SUB), :, cols] = got.reshape(LANE // SUB, SUB, n)
        dead = jnp.where(ok, 0.0, NEG)
        for b in range(n // LANE):
            colpot[k * (n // LANE) + b] = jnp.broadcast_to(dead[:, b * LANE : (b + 1) * LANE], (SUB, LANE))

    each(nc, take)
    target = stats[nc]
    both = jnp.sum(jnp.where(lane < pc, source * target, 0.0), axis=1, keepdims=True)
    total = ntgt_f * pick(source, pc) + nsrc_f * pick(target, pc) - 2.0 * both
    cbar = total / (nsrc_f * ntgt_f)
    scale = jnp.broadcast_to(-UNIT / cbar, (SUB, LANE))
    sub_row = lax.broadcasted_iota(jnp.int32, (SUB, LANE), 0)

    def rows_pass(first):
        @pl.loop(0, tiles // 4)
        def _(i):
            for u in range(4):
                r = i * 4 + u
                scores = []
                for j in range(blocks):
                    piece = cost[r, :, j * LANE : (j + 1) * LANE]
                    if first:
                        piece = piece * scale
                        cost[r, :, j * LANE : (j + 1) * LANE] = piece
                    scores.append(piece + colpot[j])
                top = tree(jnp.maximum, scores)
                row_max[r] = top
                row_sum[r] = tree(jnp.add, [jnp.exp2(s - top) for s in scores])

    def rows_lse(r):
        top = jnp.max(row_max[r], axis=1, keepdims=True)
        add = jnp.sum(row_sum[r] * jnp.exp2(row_max[r] - top), axis=1, keepdims=True)
        return top + jnp.log(add) * LOG2E

    def rows_end():
        @pl.loop(0, tiles // 16)
        def _(i):
            for u in range(16):
                r = i * 16 + u
                fpot = FI * (level[r] - rows_lse(r))
                pot[r] = jnp.where(sub_row + r * SUB < mine, fpot, NEG)

    def cols_pass(it):
        @pl.loop(0, blocks // 2)
        def _(i):
            for b in range(2):
                j = i * 2 + b
                cols = pl.ds(pl.multiple_of(j * LANE, LANE), LANE)
                tops = [None] * 4
                for r in range(tiles):
                    s = pot[r] + cost[r, :, cols]
                    tops[r % 4] = s if r < 4 else jnp.maximum(tops[r % 4], s)
                top = tree(jnp.maximum, tops)
                sums = [None] * 4
                for r in range(tiles):
                    e = jnp.exp2(pot[r] + cost[r, :, cols] - top)
                    sums[r % 4] = e if r < 4 else sums[r % 4] + e
                add = tree(jnp.add, sums)
                most = jnp.max(top, axis=0, keepdims=True)
                add = jnp.sum(add * jnp.exp2(top - most), axis=0, keepdims=True)
                parts[it, c, pl.ds(j, 1)] = most + jnp.log(add) * LOG2E

    def part_copy(it, step, slot):
        return pltpu.make_async_remote_copy(
            parts.at[it, slot], parts.at[it, slot], p_send.at[it, step], p_recv.at[it, slot],
            device_id={"tm": t, "cell": peer(step)}, device_id_type=MESH)

    cell_at = (lax.broadcasted_iota(jnp.int32, (blocks, LANE), 0) * LANE
               + lax.broadcasted_iota(jnp.int32, (blocks, LANE), 1))

    def exchange(it):
        for step in range(1, nc):
            part_copy(it, step, c).start()
        for step in range(1, nc):
            part_copy(it, step, peer(step)).wait_recv()
        pieces = [parts[it, k] for k in range(nc)]
        top = tree(jnp.maximum, pieces)
        add = tree(jnp.add, [jnp.exp2(p - top) for p in pieces])
        hpot = jnp.where(cell_at < ntgt, -FJ * (top + jnp.log(add) * LOG2E), NEG)
        for j in range(blocks):
            colpot[j] = jnp.broadcast_to(hpot[j : j + 1], (SUB, LANE))

    def one(it, first):
        rows_pass(first)
        rows_end()
        cols_pass(it)
        exchange(it)

    one(0, True)

    @pl.loop(1, ITERS)
    def _(it):
        one(it, False)

    rows_pass(False)
    per = LANE // SUB
    for k in range(n // LANE):
        fpot = pot[k * per : (k + 1) * per].reshape(LANE, LANE)
        ok = lax.broadcasted_iota(jnp.int32, (LANE, LANE), 0) + k * LANE < mine
        lse = jnp.concatenate([jnp.broadcast_to(rows_lse(k * per + r), (SUB, LANE)) for r in range(per)], axis=0)
        mass = jnp.where(ok, jnp.exp2(fpot + lse), 0.0)
        fout[:, k * LANE : (k + 1) * LANE] = jnp.where(ok, fpot * (1.0 / UNIT), 0.0).T[0:1]
        mout[:, k * LANE : (k + 1) * LANE] = mass.T[0:1]
        j = c * (n // LANE) + k
        own = colpot[j][0:1]
        good = lane + j * LANE < ntgt
        hout[:, k * LANE : (k + 1) * LANE] = jnp.where(good, own * (1.0 / UNIT), 0.0)

    for step in range(1, nc):
        stat_copy(step, c).wait_send()
        for it in range(ITERS):
            part_copy(it, step, c).wait_send()

    @pl.when(t > 0)
    def _():
        for step in range(nc):
            tgt_copy(step).wait_send()

    @pl.when(t == nt - 1)
    def _():
        for step in range(1, nc):
            last_copy(step).wait_send()


def local(points, last_points, counts, bins, rates):
    nt = lax.axis_size("tm")
    nc = lax.axis_size("cell")
    pc, n = last_points.shape
    cells = nc * n
    f32 = jnp.float32
    vmem = pl.BlockSpec(memory_space=pltpu.VMEM)
    smem = pl.BlockSpec(memory_space=pltpu.SMEM)
    row = jax.ShapeDtypeStruct((1, n), f32)
    tile = pltpu.VMEM((n // SUB, SUB, LANE), f32)
    dma = pltpu.SemaphoreType.DMA
    return pl.pallas_call(
        functools.partial(kernel, nt, nc),
        out_shape=(row, row, row),
        in_specs=[vmem, vmem, smem, vmem, smem],
        out_specs=(vmem, vmem, vmem),
        scratch_shapes=[
            pltpu.VMEM((n // SUB, SUB, cells), f32),
            pltpu.VMEM((nc, pc, n), f32),
            pltpu.VMEM((nc + 1, 1, LANE), f32),
            pltpu.VMEM((ITERS, nc, cells // LANE, LANE), f32),
            pltpu.VMEM((n, 6 * (pc + 2)), jnp.bfloat16),
            tile, tile, tile, tile,
            pltpu.VMEM((cells // LANE, SUB, LANE), f32),
            dma((nc,)), dma((nc,)), dma((nc,)), dma((nc,)), dma((nc,)),
            dma((ITERS, nc)), dma((ITERS, nc)),
        ],
        compiler_params=pltpu.CompilerParams(
            collective_id=0, has_side_effects=True, vmem_limit_bytes=48 * 1024 * 1024
        ),
        name="coupling",
    )(points, last_points, counts, bins, rates)


def solution(mesh):
    return jax.shard_map(
        local,
        mesh=mesh,
        in_specs=(P("tm", None, "cell"), P(None, "cell"), P(), P("tm", "cell"), P("tm", None)),
        out_specs=(P("tm", "cell"), P("tm", "cell"), P("tm", "cell")),
        check_vma=False,
    )
```

time: 195 us -> 39.1 us (0.20)
  blocking collectives: 81.8 us -> 0 us
  matrix products: 55.3 us -> 0 us
  Pallas kernels: 0 us -> 35.6 us
  other arithmetic: 31.8 us -> 0 us
  local copies, waits for them, and re-layouts: 17.8 us -> 2.62 us
  between operations: 3.61 us -> 0.69 us
    all_gather x9 -> x0, blocking collectives: 72.2 us -> none  [the longest x8 61.4 us: joined(): pieces = jax.tree.map(lambda part: lax.all_gather(part, axis), value)]
    dot_general x40 -> x0, matrix products: 55.3 us -> none  [raw_cost(): cross = jnp.dot(xblock.T, targets, precision=lax.Precision.HIGHEST)]
    pallas_call x0 -> x1, Pallas kernels: none -> 35.6 us  [local(): pl.pallas_call(functools.partial(kernel, nt, nc), out_shape=(row, row, ro...]
    lt x25 -> x0, other arithmetic: 14.2 us -> none  [the longest x24 13.6 us: local(): live_cols = jnp.arange(cells, dtype=jnp.int32) < ntgt]
    reduce_sum x41 -> x0, other arithmetic: 10.8 us -> none  [the longest x20 6.13 us: row_one_block(): return top + jnp.log(jnp.sum(jnp.exp(score - top[:, None]), axis=1))]
    psum x1 -> x0, blocking collectives: 9.61 us -> none  [local(): growth_sum = lax.psum(growth_part, 'cell')]
    select_n x10 -> x0, other arithmetic: 6.09 us -> none  [the longest x4 2.58 us: local(): jnp.where(live_rows, FI * (EPS * loga - EPS * row_lse(zero_rows, hfull)),...]
    slice x38 -> x0, local copies, waits for them, and re-layouts: 4.87 us -> none  [the longest x16 2.75 us: joined(): head = jax.tree.map(lambda part: part[0], pieces)]
  transfers between devices with their start and end apart: 1 -> 0, of which waited for: 0 -> 0; matrix products, arithmetic and copies ran while one was open for 1% -> 0% of each run, Pallas kernels for 0% -> 0%
where the time goes in v1:
time: 39.1 us; the launch traced here: 38.9 us
  Pallas kernels  35.6 us (91%)
  local copies, waits for them, and re-layouts  2.62 us (7%)
  between operations  0.69 us (2%)
    pallas_call x1, Pallas kernels, local(): pl.pallas_call(functools.partial(kernel, nt, nc), out_shape=(row, row, ro...  35.6 us
    unnamed x12, local copies, waits for them, and re-layouts  2.62 us

profile of v1, /device:TPU:0, one launch (start us, length us, event | category | flops | bytes accessed | tf_op | source)
XLA Modules:
  0.0 38.9 jit_solution(6549031776896857894)
XLA Ops:
  0.6 0.0 copy-start.3
  0.6 0.0 copy-start.1
  0.7 0.0 copy-start.2
  0.7 0.0 copy-start
  0.7 0.9 %copy.8.points = f32[1,30,512]{2,1,0:T(8,128)S(1)} copy(f32[1,30,512]{2,0,1:T(1,128)} %param.5) | data formatting | bytes 122880 | tf_op args[0]
  1.5 0.0 copy-done.3
  1.5 0.0 copy-done.1
  1.5 0.0 copy-done.2
  1.6 0.0 copy-done
  1.6 35.6 %coupling.1 = (f32[1,512]{1,0:T(1,128)S(1)}, f32[1,512]{1,0:T(1,128)S(1)}, f32[1,512]{1,0:T(1,128)S(1)}) custom-call(f32[1,30,512]{2,1,0:T(8,128)S(1)} %copy.8.points, f32[30,512]{1,0:T(8,128)S(1)} %copy-done, s32[9]{0:T(128)S(1)} %copy-done.2, s32[1,512]{1,0:T(1,128)S(1)} %copy-done.1, f32[1,16]{1,0:T(1,128)S(1)} %copy-done.3), custom_call_target="tpu_custom_call" | custom-call | tf_op jit(solution)/shard_map/coupling/pallas_call | solution.py:295
  37.2 0.6 %copy.12 = f32[1,512]{1,0:T(1,128)} copy(f32[1,512]{1,0:T(1,128)S(1)} %get-tuple-element.6) | data formatting | bytes 4096
  37.8 0.6 %copy.13 = f32[1,512]{1,0:T(1,128)} copy(f32[1,512]{1,0:T(1,128)S(1)} %get-tuple-element.7) | data formatting | bytes 4096
  38.4 0.6 %copy.14 = f32[1,512]{1,0:T(1,128)} copy(f32[1,512]{1,0:T(1,128)S(1)} %get-tuple-element.8) | data formatting | bytes 4096
Async XLA Ops:
  0.6 0.9 %copy-start.3 = (f32[1,16]{1,0:T(1,128)S(1)}, f32[1,16]{1,0:T(1,128)}, u32[]{:S(2)}) copy-start(f32[1,16]{1,0:T(1,128)} %rates.1) | copy-start | bytes 196
  0.6 0.9 %copy-start.1 = (s32[1,512]{1,0:T(1,128)S(1)}, s32[1,512]{1,0:T(1,128)}, u32[]{:S(2)}) copy-start(s32[1,512]{1,0:T(1,128)} %bins.1) | copy-start | bytes 6148
  0.7 0.9 %copy-start.2 = (s32[9]{0:T(128)S(1)}, s32[9]{0:T(128)}, u32[]{:S(2)}) copy-start(s32[9]{0:T(128)} %counts.1) | copy-start | bytes 112
  0.7 0.9 %copy-start = (f32[30,512]{1,0:T(8,128)S(1)}, f32[30,512]{1,0:T(8,128)}, u32[]{:S(2)}) copy-start(f32[30,512]{1,0:T(8,128)} %last.1) | copy-start | bytes 184324

commit v2 on v1

--- a/solution.py
+++ b/solution.py
@@ -18,6 +18,9 @@
 UNIT = LOG2E / EPS
 
 LANE = 128
+HALVES = 2
+GROUP = 8
+WIDE = 4
 SUB = 8
 MESH = pl.DeviceIdType.MESH
 
@@ -170,105 +173,132 @@
     scale = jnp.broadcast_to(-UNIT / cbar, (SUB, LANE))
     sub_row = lax.broadcasted_iota(jnp.int32, (SUB, LANE), 0)
 
-    def rows_pass(first):
-        @pl.loop(0, tiles // 4)
-        def _(i):
-            for u in range(4):
-                r = i * 4 + u
-                scores = []
-                for j in range(blocks):
-                    piece = cost[r, :, j * LANE : (j + 1) * LANE]
-                    if first:
-                        piece = piece * scale
-                        cost[r, :, j * LANE : (j + 1) * LANE] = piece
-                    scores.append(piece + colpot[j])
-                top = tree(jnp.maximum, scores)
-                row_max[r] = top
-                row_sum[r] = tree(jnp.add, [jnp.exp2(s - top) for s in scores])
-
-    def rows_lse(r):
+    half = blocks // HALVES
+
+    def rows_part(r, h, first):
+        scores = []
+        for j in range(h * half, (h + 1) * half):
+            piece = cost[r, :, j * LANE : (j + 1) * LANE]
+            if first:
+                piece = piece * scale
+                cost[r, :, j * LANE : (j + 1) * LANE] = piece
+            scores.append(piece + colpot[j])
+        top = tree(jnp.maximum, scores)
+        if h > 0:
+            before = row_max[r]
+            top = jnp.maximum(top, before)
+        add = tree(jnp.add, [jnp.exp2(s - top) for s in scores])
+        if h > 0:
+            add += row_sum[r] * jnp.exp2(before - top)
+        row_max[r] = top
+        row_sum[r] = add
+
+    def rows_end(r, final):
         top = jnp.max(row_max[r], axis=1, keepdims=True)
         add = jnp.sum(row_sum[r] * jnp.exp2(row_max[r] - top), axis=1, keepdims=True)
-        return top + jnp.log(add) * LOG2E
-
-    def rows_end():
-        @pl.loop(0, tiles // 16)
+        lse = top + jnp.log(add) * LOG2E
+        if final:
+            level[r] = jnp.exp2(pot[r] + lse)
+        else:
+            pot[r] = jnp.where(sub_row + r * SUB < mine, FI * (level[r] - lse), NEG)
+
+    def rows_open(h, first):
+        @pl.loop(0, tiles // GROUP)
         def _(i):
-            for u in range(16):
-                r = i * 16 + u
-                fpot = FI * (level[r] - rows_lse(r))
-                pot[r] = jnp.where(sub_row + r * SUB < mine, fpot, NEG)
-
-    def cols_pass(it):
-        @pl.loop(0, blocks // 2)
+            for u in range(GROUP):
+                rows_part(i * GROUP + u, h, first)
+
+    def rows_close(h, first, final):
+        for u in range(GROUP):
+            rows_part(u, h, first)
+
+        @pl.loop(1, tiles // GROUP)
         def _(i):
-            for b in range(2):
-                j = i * 2 + b
-                cols = pl.ds(pl.multiple_of(j * LANE, LANE), LANE)
-                tops = [None] * 4
-                for r in range(tiles):
-                    s = pot[r] + cost[r, :, cols]
-                    tops[r % 4] = s if r < 4 else jnp.maximum(tops[r % 4], s)
-                top = tree(jnp.maximum, tops)
-                sums = [None] * 4
-                for r in range(tiles):
-                    e = jnp.exp2(pot[r] + cost[r, :, cols] - top)
-                    sums[r % 4] = e if r < 4 else sums[r % 4] + e
-                add = tree(jnp.add, sums)
-                most = jnp.max(top, axis=0, keepdims=True)
-                add = jnp.sum(add * jnp.exp2(top - most), axis=0, keepdims=True)
-                parts[it, c, pl.ds(j, 1)] = most + jnp.log(add) * LOG2E
-
-    def part_copy(it, step, slot):
+            for u in range(GROUP):
+                rows_end((i - 1) * GROUP + u, final)
+            for u in range(GROUP):
+                rows_part(i * GROUP + u, h, first)
+
+        for u in range(GROUP):
+            rows_end(tiles - GROUP + u, final)
+
+    def cols_part(it, h):
+        @pl.loop(0, half // WIDE)
+        def _(i):
+            at = [pl.multiple_of((h * half + i * WIDE + b) * LANE, LANE) for b in range(WIDE)]
+            tops = [[None, None] for _ in at]
+            for r in range(tiles):
+                base = pot[r]
+                for b in range(WIDE):
+                    s = base + cost[r, :, pl.ds(at[b], LANE)]
+                    tops[b][r % 2] = s if r < 2 else jnp.maximum(tops[b][r % 2], s)
+            top = [jnp.maximum(*pair) for pair in tops]
+            sums = [[None, None] for _ in at]
+            for r in range(tiles):
+                base = pot[r]
+                for b in range(WIDE):
+                    e = jnp.exp2(base + cost[r, :, pl.ds(at[b], LANE)] - top[b])
+                    sums[b][r % 2] = e if r < 2 else sums[b][r % 2] + e
+            for b in range(WIDE):
+                most = jnp.max(top[b], axis=0, keepdims=True)
+                add = (sums[b][0] + sums[b][1]) * jnp.exp2(top[b] - most)
+                lse = most + jnp.log(jnp.sum(add, axis=0, keepdims=True)) * LOG2E
+                parts[it, c, h, pl.ds(i * WIDE + b, 1)] = lse
+
+    def part_copy(it, step, slot, h):
         return pltpu.make_async_remote_copy(
-            parts.at[it, slot], parts.at[it, slot], p_send.at[it, step], p_recv.at[it, slot],
+            parts.at[it, slot, h], parts.at[it, slot, h], p_send.at[it, step, h], p_recv.at[it, slot, h],
             device_id={"tm": t, "cell": peer(step)}, device_id_type=MESH)
 
-    cell_at = (lax.broadcasted_iota(jnp.int32, (blocks, LANE), 0) * LANE
-               + lax.broadcasted_iota(jnp.int32, (blocks, LANE), 1))
-
-    def exchange(it):
+    cell_at = (lax.broadcasted_iota(jnp.int32, (half, LANE), 0) * LANE
+               + lax.broadcasted_iota(jnp.int32, (half, LANE), 1))
+
+    def joined(it, h):
         for step in range(1, nc):
-            part_copy(it, step, c).start()
-        for step in range(1, nc):
-            part_copy(it, step, peer(step)).wait_recv()
-        pieces = [parts[it, k] for k in range(nc)]
+            part_copy(it, step, peer(step), h).wait_recv()
+        pieces = [parts[it, k, h] for k in range(nc)]
         top = tree(jnp.maximum, pieces)
         add = tree(jnp.add, [jnp.exp2(p - top) for p in pieces])
-        hpot = jnp.where(cell_at < ntgt, -FJ * (top + jnp.log(add) * LOG2E), NEG)
-        for j in range(blocks):
-            colpot[j] = jnp.broadcast_to(hpot[j : j + 1], (SUB, LANE))
-
-    def one(it, first):
-        rows_pass(first)
-        rows_end()
-        cols_pass(it)
-        exchange(it)
-
-    one(0, True)
-
-    @pl.loop(1, ITERS)
+        ok = cell_at < ntgt - h * half * LANE
+        hpot = jnp.where(ok, -FJ * (top + jnp.log(add) * LOG2E), NEG)
+        for j in range(half):
+            colpot[h * half + j] = jnp.broadcast_to(hpot[j : j + 1], (SUB, LANE))
+
+    def one(it, final):
+        for h in range(HALVES):
+            cols_part(it, h)
+            for step in range(1, nc):
+                part_copy(it, step, c, h).start()
+        joined(it, 0)
+        rows_open(0, False)
+        joined(it, 1)
+        rows_close(1, False, final)
+
+    rows_open(0, True)
+    rows_close(1, True, False)
+
+    @pl.loop(0, ITERS - 1)
     def _(it):
         one(it, False)
 
-    rows_pass(False)
+    one(ITERS - 1, True)
     per = LANE // SUB
     for k in range(n // LANE):
-        fpot = pot[k * per : (k + 1) * per].reshape(LANE, LANE)
-        ok = lax.broadcasted_iota(jnp.int32, (LANE, LANE), 0) + k * LANE < mine
-        lse = jnp.concatenate([jnp.broadcast_to(rows_lse(k * per + r), (SUB, LANE)) for r in range(per)], axis=0)
-        mass = jnp.where(ok, jnp.exp2(fpot + lse), 0.0)
-        fout[:, k * LANE : (k + 1) * LANE] = jnp.where(ok, fpot * (1.0 / UNIT), 0.0).T[0:1]
-        mout[:, k * LANE : (k + 1) * LANE] = mass.T[0:1]
+        cols = slice(k * LANE, (k + 1) * LANE)
+        ok = lane + k * LANE < mine
+        fpot = pot[k * per : (k + 1) * per].reshape(LANE, LANE).T[0:1]
+        mass = level[k * per : (k + 1) * per].reshape(LANE, LANE).T[0:1]
+        fout[:, cols] = jnp.where(ok, fpot * (1.0 / UNIT), 0.0)
+        mout[:, cols] = jnp.where(ok, mass, 0.0)
         j = c * (n // LANE) + k
-        own = colpot[j][0:1]
         good = lane + j * LANE < ntgt
-        hout[:, k * LANE : (k + 1) * LANE] = jnp.where(good, own * (1.0 / UNIT), 0.0)
+        hout[:, cols] = jnp.where(good, colpot[j][0:1] * (1.0 / UNIT), 0.0)
 
     for step in range(1, nc):
         stat_copy(step, c).wait_send()
         for it in range(ITERS):
-            part_copy(it, step, c).wait_send()
+            for h in range(HALVES):
+                part_copy(it, step, c, h).wait_send()
 
     @pl.when(t > 0)
     def _():
@@ -301,12 +331,12 @@
             pltpu.VMEM((n // SUB, SUB, cells), f32),
             pltpu.VMEM((nc, pc, n), f32),
             pltpu.VMEM((nc + 1, 1, LANE), f32),
-            pltpu.VMEM((ITERS, nc, cells // LANE, LANE), f32),
+            pltpu.VMEM((ITERS, nc, HALVES, cells // LANE // HALVES, LANE), f32),
             pltpu.VMEM((n, 6 * (pc + 2)), jnp.bfloat16),
             tile, tile, tile, tile,
             pltpu.VMEM((cells // LANE, SUB, LANE), f32),
             dma((nc,)), dma((nc,)), dma((nc,)), dma((nc,)), dma((nc,)),
-            dma((ITERS, nc)), dma((ITERS, nc)),
+            dma((ITERS, nc, HALVES)), dma((ITERS, nc, HALVES)),
         ],
         compiler_params=pltpu.CompilerParams(
             collective_id=0, has_side_effects=True, vmem_limit_bytes=48 * 1024 * 1024

time: 39.1 us -> 38.8 us (level)
  no operation moved by 1% of the time
where the time goes in v2:
time: 38.8 us; the launch traced here: 38.6 us
  Pallas kernels  35.3 us (91%)
  local copies, waits for them, and re-layouts  2.62 us (7%)
  between operations  0.69 us (2%)
    pallas_call x1, Pallas kernels, local(): pl.pallas_call(functools.partial(kernel, nt, nc), out_shape=(row, row, ro...  35.3 us
    unnamed x12, local copies, waits for them, and re-layouts  2.62 us

profile of v2, /device:TPU:0, one launch (start us, length us, event | category | flops | bytes accessed | tf_op | source)
XLA Modules:
  0.0 38.6 jit_solution(9808884513550250474)
XLA Ops:
  0.6 0.0 copy-start.3
  0.6 0.0 copy-start.1
  0.7 0.0 copy-start.2
  0.7 0.0 copy-start
  0.7 0.9 %copy.8.points = f32[1,30,512]{2,1,0:T(8,128)S(1)} copy(f32[1,30,512]{2,0,1:T(1,128)} %param.5) | data formatting | bytes 122880 | tf_op args[0]
  1.5 0.0 copy-done.3
  1.5 0.0 copy-done.1
  1.5 0.0 copy-done.2
  1.6 0.0 copy-done
  1.6 35.3 %coupling.1 = (f32[1,512]{1,0:T(1,128)S(1)}, f32[1,512]{1,0:T(1,128)S(1)}, f32[1,512]{1,0:T(1,128)S(1)}) custom-call(f32[1,30,512]{2,1,0:T(8,128)S(1)} %copy.8.points, f32[30,512]{1,0:T(8,128)S(1)} %copy-done, s32[9]{0:T(128)S(1)} %copy-done.2, s32[1,512]{1,0:T(1,128)S(1)} %copy-done.1, f32[1,16]{1,0:T(1,128)S(1)} %copy-done.3), custom_call_target="tpu_custom_call" | custom-call | tf_op jit(solution)/shard_map/coupling/pallas_call | solution.py:325
  36.9 0.6 %copy.12 = f32[1,512]{1,0:T(1,128)} copy(f32[1,512]{1,0:T(1,128)S(1)} %get-tuple-element.6) | data formatting | bytes 4096
  37.5 0.6 %copy.13 = f32[1,512]{1,0:T(1,128)} copy(f32[1,512]{1,0:T(1,128)S(1)} %get-tuple-element.7) | data formatting | bytes 4096
  38.0 0.6 %copy.14 = f32[1,512]{1,0:T(1,128)} copy(f32[1,512]{1,0:T(1,128)S(1)} %get-tuple-element.8) | data formatting | bytes 4096
Async XLA Ops:
  0.6 0.9 %copy-start.3 = (f32[1,16]{1,0:T(1,128)S(1)}, f32[1,16]{1,0:T(1,128)}, u32[]{:S(2)}) copy-start(f32[1,16]{1,0:T(1,128)} %rates.1) | copy-start | bytes 196
  0.6 0.9 %copy-start.1 = (s32[1,512]{1,0:T(1,128)S(1)}, s32[1,512]{1,0:T(1,128)}, u32[]{:S(2)}) copy-start(s32[1,512]{1,0:T(1,128)} %bins.1) | copy-start | bytes 6148
  0.7 0.9 %copy-start.2 = (s32[9]{0:T(128)S(1)}, s32[9]{0:T(128)}, u32[]{:S(2)}) copy-start(s32[9]{0:T(128)} %counts.1) | copy-start | bytes 112
  0.7 0.9 %copy-start = (f32[30,512]{1,0:T(8,128)S(1)}, f32[30,512]{1,0:T(8,128)}, u32[]{:S(2)}) copy-start(f32[30,512]{1,0:T(8,128)} %last.1) | copy-start | bytes 184324

commit v3 on v2

--- a/solution.py
+++ b/solution.py
@@ -19,7 +19,7 @@
 
 LANE = 128
 HALVES = 2
-GROUP = 8
+GROUP = 16
 WIDE = 4
 SUB = 8
 MESH = pl.DeviceIdType.MESH
@@ -54,7 +54,7 @@
 
 
 def kernel(nt, nc, points, last, counts, bins, rates, fout, hout, mout,
-           cost, tgt, stats, parts, lhs, pot, row_max, row_sum, level, colpot,
+           cost, tgt, stats, parts, lhs, pot, row_max, row_sum, level, fpot, colpot,
            tgt_send, last_send, tgt_recv, st_send, st_recv, p_send, p_recv):
     t = lax.axis_index("tm")
     c = lax.axis_index("cell")
@@ -139,10 +139,7 @@
     nsrc_f = nsrc.astype(f32)
     ntgt_f = ntgt.astype(f32)
     gbar = pick(source, pc + 1) / nsrc_f
-    loga = (jnp.log(growth) - jnp.log(gbar)) * LOG2E
-    for k in range(n // LANE):
-        wide = jnp.broadcast_to(loga[:, k * LANE : (k + 1) * LANE], (LANE, LANE))
-        level[k * (LANE // SUB) : (k + 1) * (LANE // SUB)] = wide.T.reshape(LANE // SUB, SUB, LANE)
+    level[...] = (jnp.log(growth) - jnp.log(gbar)) * LOG2E
 
     colpot[...] = jnp.zeros_like(colpot)
     stats[nc] = jnp.zeros((1, LANE), f32)
@@ -171,9 +168,9 @@
     total = ntgt_f * pick(source, pc) + nsrc_f * pick(target, pc) - 2.0 * both
     cbar = total / (nsrc_f * ntgt_f)
     scale = jnp.broadcast_to(-UNIT / cbar, (SUB, LANE))
-    sub_row = lax.broadcasted_iota(jnp.int32, (SUB, LANE), 0)
 
     half = blocks // HALVES
+    per = LANE // SUB
 
     def rows_part(r, h, first):
         scores = []
@@ -193,14 +190,20 @@
         row_max[r] = top
         row_sum[r] = add
 
-    def rows_end(r, final):
-        top = jnp.max(row_max[r], axis=1, keepdims=True)
-        add = jnp.sum(row_sum[r] * jnp.exp2(row_max[r] - top), axis=1, keepdims=True)
-        lse = top + jnp.log(add) * LOG2E
+    def rows_end(k, final):
+        rows = slice(k * per, (k + 1) * per)
+        cols = slice(k * LANE, (k + 1) * LANE)
+        tops = row_max[rows].reshape(LANE, LANE).T
+        adds = row_sum[rows].reshape(LANE, LANE).T
+        top = jnp.max(tops, axis=0, keepdims=True)
+        lse = top + jnp.log(jnp.sum(adds * jnp.exp2(tops - top), axis=0, keepdims=True)) * LOG2E
+        ok = lane + k * LANE < mine
         if final:
-            level[r] = jnp.exp2(pot[r] + lse)
+            mout[:, cols] = jnp.where(ok, jnp.exp2(fpot[:, cols] + lse), 0.0)
         else:
-            pot[r] = jnp.where(sub_row + r * SUB < mine, FI * (level[r] - lse), NEG)
+            value = jnp.where(ok, FI * (level[:, cols] - lse), NEG)
+            fpot[:, cols] = value
+            pot[rows] = jnp.broadcast_to(value, (LANE, LANE)).T.reshape(per, SUB, LANE)
 
     def rows_open(h, first):
         @pl.loop(0, tiles // GROUP)
@@ -209,18 +212,9 @@
                 rows_part(i * GROUP + u, h, first)
 
     def rows_close(h, first, final):
-        for u in range(GROUP):
-            rows_part(u, h, first)
-
-        @pl.loop(1, tiles // GROUP)
-        def _(i):
-            for u in range(GROUP):
-                rows_end((i - 1) * GROUP + u, final)
-            for u in range(GROUP):
-                rows_part(i * GROUP + u, h, first)
-
-        for u in range(GROUP):
-            rows_end(tiles - GROUP + u, final)
+        rows_open(h, first)
+        for k in range(n // LANE):
+            rows_end(k, final)
 
     def cols_part(it, h):
         @pl.loop(0, half // WIDE)
@@ -282,14 +276,9 @@
         one(it, False)
 
     one(ITERS - 1, True)
-    per = LANE // SUB
     for k in range(n // LANE):
         cols = slice(k * LANE, (k + 1) * LANE)
-        ok = lane + k * LANE < mine
-        fpot = pot[k * per : (k + 1) * per].reshape(LANE, LANE).T[0:1]
-        mass = level[k * per : (k + 1) * per].reshape(LANE, LANE).T[0:1]
-        fout[:, cols] = jnp.where(ok, fpot * (1.0 / UNIT), 0.0)
-        mout[:, cols] = jnp.where(ok, mass, 0.0)
+        fout[:, cols] = jnp.where(lane + k * LANE < mine, fpot[:, cols] * (1.0 / UNIT), 0.0)
         j = c * (n // LANE) + k
         good = lane + j * LANE < ntgt
         hout[:, cols] = jnp.where(good, colpot[j][0:1] * (1.0 / UNIT), 0.0)
@@ -333,7 +322,8 @@
             pltpu.VMEM((nc + 1, 1, LANE), f32),
             pltpu.VMEM((ITERS, nc, HALVES, cells // LANE // HALVES, LANE), f32),
             pltpu.VMEM((n, 6 * (pc + 2)), jnp.bfloat16),
-            tile, tile, tile, tile,
+            tile, tile, tile,
+            pltpu.VMEM((1, n), f32), pltpu.VMEM((1, n), f32),
             pltpu.VMEM((cells // LANE, SUB, LANE), f32),
             dma((nc,)), dma((nc,)), dma((nc,)), dma((nc,)), dma((nc,)),
             dma((ITERS, nc, HALVES)), dma((ITERS, nc, HALVES)),

time: 38.8 us -> 34.5 us (0.89)
  Pallas kernels: 35.3 us -> 31 us
    pallas_call x1, Pallas kernels: 35.3 us -> 31 us  [local(): pl.pallas_call(functools.partial(kernel, nt, nc), out_shape=(row, row, ro...]
where the time goes in v3:
time: 34.5 us; the launch traced here: 34.3 us
  Pallas kernels  31 us (90%)
  local copies, waits for them, and re-layouts  2.62 us (8%)
  between operations  0.69 us (2%)
    pallas_call x1, Pallas kernels, local(): pl.pallas_call(functools.partial(kernel, nt, nc), out_shape=(row, row, ro...  31 us
    unnamed x12, local copies, waits for them, and re-layouts  2.62 us

profile of v3, /device:TPU:0, one launch (start us, length us, event | category | flops | bytes accessed | tf_op | source)
XLA Modules:
  0.0 34.3 jit_solution(13902966569815761962)
XLA Ops:
  0.6 0.0 copy-start.3
  0.6 0.0 copy-start.1
  0.7 0.0 copy-start.2
  0.7 0.0 copy-start
  0.7 0.9 %copy.8.points = f32[1,30,512]{2,1,0:T(8,128)S(1)} copy(f32[1,30,512]{2,0,1:T(1,128)} %param.5) | data formatting | bytes 122880 | tf_op args[0]
  1.5 0.0 copy-done.3
  1.5 0.0 copy-done.1
  1.5 0.0 copy-done.2
  1.6 0.0 copy-done
  1.6 31.0 %coupling.1 = (f32[1,512]{1,0:T(1,128)S(1)}, f32[1,512]{1,0:T(1,128)S(1)}, f32[1,512]{1,0:T(1,128)S(1)}) custom-call(f32[1,30,512]{2,1,0:T(8,128)S(1)} %copy.8.points, f32[30,512]{1,0:T(8,128)S(1)} %copy-done, s32[9]{0:T(128)S(1)} %copy-done.2, s32[1,512]{1,0:T(1,128)S(1)} %copy-done.1, f32[1,16]{1,0:T(1,128)S(1)} %copy-done.3), custom_call_target="tpu_custom_call" | custom-call | tf_op jit(solution)/shard_map/coupling/pallas_call | solution.py:314
  32.6 0.6 %copy.12 = f32[1,512]{1,0:T(1,128)} copy(f32[1,512]{1,0:T(1,128)S(1)} %get-tuple-element.6) | data formatting | bytes 4096
  33.2 0.6 %copy.13 = f32[1,512]{1,0:T(1,128)} copy(f32[1,512]{1,0:T(1,128)S(1)} %get-tuple-element.7) | data formatting | bytes 4096
  33.7 0.6 %copy.14 = f32[1,512]{1,0:T(1,128)} copy(f32[1,512]{1,0:T(1,128)S(1)} %get-tuple-element.8) | data formatting | bytes 4096
Async XLA Ops:
  0.6 0.9 %copy-start.3 = (f32[1,16]{1,0:T(1,128)S(1)}, f32[1,16]{1,0:T(1,128)}, u32[]{:S(2)}) copy-start(f32[1,16]{1,0:T(1,128)} %rates.1) | copy-start | bytes 196
  0.6 0.9 %copy-start.1 = (s32[1,512]{1,0:T(1,128)S(1)}, s32[1,512]{1,0:T(1,128)}, u32[]{:S(2)}) copy-start(s32[1,512]{1,0:T(1,128)} %bins.1) | copy-start | bytes 6148
  0.7 0.9 %copy-start.2 = (s32[9]{0:T(128)S(1)}, s32[9]{0:T(128)}, u32[]{:S(2)}) copy-start(s32[9]{0:T(128)} %counts.1) | copy-start | bytes 112
  0.7 0.9 %copy-start = (f32[30,512]{1,0:T(8,128)S(1)}, f32[30,512]{1,0:T(8,128)}, u32[]{:S(2)}) copy-start(f32[30,512]{1,0:T(8,128)} %last.1) | copy-start | bytes 184324

commit v4 on v3

--- a/solution.py
+++ b/solution.py
@@ -54,7 +54,7 @@
 
 
 def kernel(nt, nc, points, last, counts, bins, rates, fout, hout, mout,
-           cost, tgt, stats, parts, lhs, pot, row_max, row_sum, level, fpot, colpot,
+           cost, tgt, stats, sums, parts, lhs, pot, row_max, row_sum, level, fpot, colpot,
            tgt_send, last_send, tgt_recv, st_send, st_recv, p_send, p_recv):
     t = lax.axis_index("tm")
     c = lax.axis_index("cell")
@@ -87,9 +87,6 @@
     for k in range(rates.shape[1]):
         growth = jnp.where(bins[...] == k, rates[0, k], growth)
     stats[c] = lane_totals(jnp.concatenate([x, sqx, jnp.where(live, growth, 0.0)], axis=0))
-    x1, x2, x3 = splits(jnp.concatenate([-2.0 * x, sqx, jnp.ones((1, n), f32)], axis=0))
-    stacked = jnp.concatenate([x1, x1, x2, x2, x1, x3], axis=0)
-    lhs[...] = stacked.T
 
     @pl.when(t == 0)
     def _():
@@ -128,6 +125,10 @@
             last_copy(step).start()
         pltpu.make_async_copy(last, tgt.at[c], tgt_recv.at[c]).start()
 
+    x1, x2, x3 = splits(jnp.concatenate([-2.0 * x, sqx, jnp.ones((1, n), f32)], axis=0))
+    stacked = jnp.concatenate([x1, x1, x2, x2, x1, x3], axis=0)
+    lhs[...] = stacked.T
+
     for step in range(1, nc):
         stat_copy(step, peer(step)).wait_recv()
     source = tree(jnp.add, [stats[k] for k in range(nc)])
@@ -142,7 +143,7 @@
     level[...] = (jnp.log(growth) - jnp.log(gbar)) * LOG2E
 
     colpot[...] = jnp.zeros_like(colpot)
-    stats[nc] = jnp.zeros((1, LANE), f32)
+    sums[...] = jnp.zeros_like(sums)
 
     def take(step):
         k = peer(step)
@@ -151,19 +152,19 @@
         y = jnp.where(ok, tgt[k], 0.0)
         sqy = jnp.sum(y * y, axis=0, keepdims=True)
         one = jnp.ones((1, n), f32)
-        stats[nc] += lane_totals(jnp.concatenate([y, sqy, jnp.zeros((1, n), f32)], axis=0))
+        both = jnp.concatenate([y, sqy, jnp.zeros((1, n), f32)], axis=0)
+        sums[...] += tree(jnp.add, [both[:, i : i + LANE] for i in range(0, n, LANE)])
         y1, y2, y3 = splits(jnp.concatenate([y, one, sqy], axis=0))
         rhs = jnp.concatenate([y1, y2, y1, y2, y3, y1], axis=0)
         cols = pl.ds(pl.multiple_of(k * n, LANE), n)
-        for rb in range(n // LANE):
-            got = jnp.dot(lhs[rb * LANE : (rb + 1) * LANE], rhs, preferred_element_type=f32)
-            cost[rb * (LANE // SUB) : (rb + 1) * (LANE // SUB), :, cols] = got.reshape(LANE // SUB, SUB, n)
+        got = jnp.dot(lhs[...], rhs, preferred_element_type=f32)
+        cost[:, :, cols] = got.reshape(tiles, SUB, n)
         dead = jnp.where(ok, 0.0, NEG)
         for b in range(n // LANE):
             colpot[k * (n // LANE) + b] = jnp.broadcast_to(dead[:, b * LANE : (b + 1) * LANE], (SUB, LANE))
 
     each(nc, take)
-    target = stats[nc]
+    target = lane_totals(sums[...])
     both = jnp.sum(jnp.where(lane < pc, source * target, 0.0), axis=1, keepdims=True)
     total = ntgt_f * pick(source, pc) + nsrc_f * pick(target, pc) - 2.0 * both
     cbar = total / (nsrc_f * ntgt_f)
@@ -227,15 +228,15 @@
                     s = base + cost[r, :, pl.ds(at[b], LANE)]
                     tops[b][r % 2] = s if r < 2 else jnp.maximum(tops[b][r % 2], s)
             top = [jnp.maximum(*pair) for pair in tops]
-            sums = [[None, None] for _ in at]
+            adds = [[None, None] for _ in at]
             for r in range(tiles):
                 base = pot[r]
                 for b in range(WIDE):
                     e = jnp.exp2(base + cost[r, :, pl.ds(at[b], LANE)] - top[b])
-                    sums[b][r % 2] = e if r < 2 else sums[b][r % 2] + e
+                    adds[b][r % 2] = e if r < 2 else adds[b][r % 2] + e
             for b in range(WIDE):
                 most = jnp.max(top[b], axis=0, keepdims=True)
-                add = (sums[b][0] + sums[b][1]) * jnp.exp2(top[b] - most)
+                add = (adds[b][0] + adds[b][1]) * jnp.exp2(top[b] - most)
                 lse = most + jnp.log(jnp.sum(add, axis=0, keepdims=True)) * LOG2E
                 parts[it, c, h, pl.ds(i * WIDE + b, 1)] = lse
 
@@ -319,7 +320,8 @@
         scratch_shapes=[
             pltpu.VMEM((n // SUB, SUB, cells), f32),
             pltpu.VMEM((nc, pc, n), f32),
-            pltpu.VMEM((nc + 1, 1, LANE), f32),
+            pltpu.VMEM((nc, 1, LANE), f32),
+            pltpu.VMEM((pc + 2, LANE), f32),
             pltpu.VMEM((ITERS, nc, HALVES, cells // LANE // HALVES, LANE), f32),
             pltpu.VMEM((n, 6 * (pc + 2)), jnp.bfloat16),
             tile, tile, tile,

time: 34.5 us -> 34.5 us (level)
  no operation moved by 1% of the time
where the time goes in v4:
time: 34.5 us; the launch traced here: 34.3 us
  Pallas kernels  31 us (90%)
  local copies, waits for them, and re-layouts  2.62 us (8%)
  between operations  0.69 us (2%)
    pallas_call x1, Pallas kernels, local(): pl.pallas_call(functools.partial(kernel, nt, nc), out_shape=(row, row, ro...  31 us
    unnamed x12, local copies, waits for them, and re-layouts  2.62 us

profile of v4, /device:TPU:0, one launch (start us, length us, event | category | flops | bytes accessed | tf_op | source)
XLA Modules:
  0.0 34.3 jit_solution(7682960353104242837)
XLA Ops:
  0.6 0.0 copy-start.3
  0.6 0.0 copy-start.1
  0.7 0.0 copy-start.2
  0.7 0.0 copy-start
  0.7 0.9 %copy.8.points = f32[1,30,512]{2,1,0:T(8,128)S(1)} copy(f32[1,30,512]{2,0,1:T(1,128)} %param.5) | data formatting | bytes 122880 | tf_op args[0]
  1.5 0.0 copy-done.3
  1.5 0.0 copy-done.1
  1.5 0.0 copy-done.2
  1.6 0.0 copy-done
  1.6 31.0 %coupling.1 = (f32[1,512]{1,0:T(1,128)S(1)}, f32[1,512]{1,0:T(1,128)S(1)}, f32[1,512]{1,0:T(1,128)S(1)}) custom-call(f32[1,30,512]{2,1,0:T(8,128)S(1)} %copy.8.points, f32[30,512]{1,0:T(8,128)S(1)} %copy-done, s32[9]{0:T(128)S(1)} %copy-done.2, s32[1,512]{1,0:T(1,128)S(1)} %copy-done.1, f32[1,16]{1,0:T(1,128)S(1)} %copy-done.3), custom_call_target="tpu_custom_call" | custom-call | tf_op jit(solution)/shard_map/coupling/pallas_call | solution.py:315
  32.6 0.6 %copy.12 = f32[1,512]{1,0:T(1,128)} copy(f32[1,512]{1,0:T(1,128)S(1)} %get-tuple-element.6) | data formatting | bytes 4096
  33.2 0.6 %copy.13 = f32[1,512]{1,0:T(1,128)} copy(f32[1,512]{1,0:T(1,128)S(1)} %get-tuple-element.7) | data formatting | bytes 4096
  33.7 0.6 %copy.14 = f32[1,512]{1,0:T(1,128)} copy(f32[1,512]{1,0:T(1,128)S(1)} %get-tuple-element.8) | data formatting | bytes 4096
Async XLA Ops:
  0.6 0.9 %copy-start.3 = (f32[1,16]{1,0:T(1,128)S(1)}, f32[1,16]{1,0:T(1,128)}, u32[]{:S(2)}) copy-start(f32[1,16]{1,0:T(1,128)} %rates.1) | copy-start | bytes 196
  0.6 0.9 %copy-start.1 = (s32[1,512]{1,0:T(1,128)S(1)}, s32[1,512]{1,0:T(1,128)}, u32[]{:S(2)}) copy-start(s32[1,512]{1,0:T(1,128)} %bins.1) | copy-start | bytes 6148
  0.7 0.9 %copy-start.2 = (s32[9]{0:T(128)S(1)}, s32[9]{0:T(128)}, u32[]{:S(2)}) copy-start(s32[9]{0:T(128)} %counts.1) | copy-start | bytes 112
  0.7 0.9 %copy-start = (f32[30,512]{1,0:T(8,128)S(1)}, f32[30,512]{1,0:T(8,128)}, u32[]{:S(2)}) copy-start(f32[30,512]{1,0:T(8,128)} %last.1) | copy-start | bytes 184324

commit v5 on v4

--- a/solution.py
+++ b/solution.py
@@ -19,8 +19,8 @@
 
 LANE = 128
 HALVES = 2
-GROUP = 16
-WIDE = 4
+GROUP = 32
+WIDE = 8
 SUB = 8
 MESH = pl.DeviceIdType.MESH
 

time: 34.5 us -> 33.2 us (0.962)
  Pallas kernels: 31 us -> 29.7 us
    pallas_call x1, Pallas kernels: 31 us -> 29.7 us  [local(): pl.pallas_call(functools.partial(kernel, nt, nc), out_shape=(row, row, ro...]
where the time goes in v5:
time: 33.2 us; the launch traced here: 33.1 us
  Pallas kernels  29.7 us (89%)
  local copies, waits for them, and re-layouts  2.62 us (8%)
  between operations  0.69 us (2%)
    pallas_call x1, Pallas kernels, local(): pl.pallas_call(functools.partial(kernel, nt, nc), out_shape=(row, row, ro...  29.7 us
    unnamed x12, local copies, waits for them, and re-layouts  2.62 us

profile of v5, /device:TPU:0, one launch (start us, length us, event | category | flops | bytes accessed | tf_op | source)
XLA Modules:
  0.0 33.1 jit_solution(16710862598668105703)
XLA Ops:
  0.6 0.0 copy-start.3
  0.6 0.0 copy-start.1
  0.7 0.0 copy-start.2
  0.7 0.0 copy-start
  0.7 0.9 %copy.8.points = f32[1,30,512]{2,1,0:T(8,128)S(1)} copy(f32[1,30,512]{2,0,1:T(1,128)} %param.5) | data formatting | bytes 122880 | tf_op args[0]
  1.5 0.0 copy-done.3
  1.5 0.0 copy-done.1
  1.5 0.0 copy-done.2
  1.6 0.0 copy-done
  1.6 29.7 %coupling.1 = (f32[1,512]{1,0:T(1,128)S(1)}, f32[1,512]{1,0:T(1,128)S(1)}, f32[1,512]{1,0:T(1,128)S(1)}) custom-call(f32[1,30,512]{2,1,0:T(8,128)S(1)} %copy.8.points, f32[30,512]{1,0:T(8,128)S(1)} %copy-done, s32[9]{0:T(128)S(1)} %copy-done.2, s32[1,512]{1,0:T(1,128)S(1)} %copy-done.1, f32[1,16]{1,0:T(1,128)S(1)} %copy-done.3), custom_call_target="tpu_custom_call" | custom-call | tf_op jit(solution)/shard_map/coupling/pallas_call | solution.py:315
  31.3 0.6 %copy.12 = f32[1,512]{1,0:T(1,128)} copy(f32[1,512]{1,0:T(1,128)S(1)} %get-tuple-element.6) | data formatting | bytes 4096
  31.9 0.6 %copy.13 = f32[1,512]{1,0:T(1,128)} copy(f32[1,512]{1,0:T(1,128)S(1)} %get-tuple-element.7) | data formatting | bytes 4096
  32.5 0.6 %copy.14 = f32[1,512]{1,0:T(1,128)} copy(f32[1,512]{1,0:T(1,128)S(1)} %get-tuple-element.8) | data formatting | bytes 4096
Async XLA Ops:
  0.6 0.9 %copy-start.3 = (f32[1,16]{1,0:T(1,128)S(1)}, f32[1,16]{1,0:T(1,128)}, u32[]{:S(2)}) copy-start(f32[1,16]{1,0:T(1,128)} %rates.1) | copy-start | bytes 196
  0.6 0.9 %copy-start.1 = (s32[1,512]{1,0:T(1,128)S(1)}, s32[1,512]{1,0:T(1,128)}, u32[]{:S(2)}) copy-start(s32[1,512]{1,0:T(1,128)} %bins.1) | copy-start | bytes 6148
  0.7 0.9 %copy-start.2 = (s32[9]{0:T(128)S(1)}, s32[9]{0:T(128)}, u32[]{:S(2)}) copy-start(s32[9]{0:T(128)} %counts.1) | copy-start | bytes 112
  0.7 0.9 %copy-start = (f32[30,512]{1,0:T(8,128)S(1)}, f32[30,512]{1,0:T(8,128)}, u32[]{:S(2)}) copy-start(f32[30,512]{1,0:T(8,128)} %last.1) | copy-start | bytes 184324
